TPU v7x, 768 devices: a whole 4x8x12 slice. The times are simulated.
768 devices in a mesh: dp: 96 (over y_lo, z, core), fsdp: 8 (over y_hi, x).
Axes of the slice: x: 4, y: 8 (y_hi: 2, y_lo: 4; y = y_hi * 4 + y_lo), z: 12, core: 2. Of those that a mesh axis runs over, the one named last changes fastest.
Arguments:
- queries: bfloat16 [49152, 3072], P('dp', 'fsdp'), may hold values from -64 to 64
- key_rows: bfloat16 [49152, 3072], P('dp', 'fsdp'), may hold values from -16 to 16
- value_rows: bfloat16 [49152, 3072], P('dp', 'fsdp'), may hold values from -6 to 6
- segments: int32 [49152], P('dp'), may hold values from 0 to 384, as said below
- send_block: int32 [384], P('dp'), may hold values from 0 to 1, as said below
- out_weight: bfloat16 [3072, 6144], P('fsdp'), may hold values from -0.15625 to 0.15625
- grad_attended: bfloat16 [49152, 3072], P('dp', 'fsdp'), may hold values from -6 to 6
Outputs:
- layer_out: bfloat16 [49152, 6144], P('dp', 'fsdp')
- grad_queries: bfloat16 [49152, 3072], P('dp', 'fsdp')
- grad_keys: bfloat16 [49152, 3072], P('dp', 'fsdp')
- grad_values: bfloat16 [49152, 3072], P('dp', 'fsdp')
Inputs may be any that keep to these rules, and one draw needn't show every extreme that they name: `segments`: each image covers one or two whole blocks of 128 rows of one index of dp and begins at its first block's first row; its id is the index of that block among all 384 blocks, and the rows after its patches carry 96 * 4. A one-block image has 64 to 128 patches, a two-block image 128 + 1 to 256. `send_block`: each index of dp marks exactly 2 of its 4 blocks, and its marked blocks hold whole images.
All inputs are finite; a program needn't handle non-finite values.
Results may differ from a plain program's by a relative error of at most 0.015.
Values may be sent and summed in bfloat16 or wider, within the bound.
A program may use at most 64 MiB of HBM per device.

v0:
```python
import math

import jax
import jax.numpy as jnp
from jax import lax
from jax.sharding import PartitionSpec as P

HD = 128
BLOCK = 128
NB = 4
MOVE = 2


def shifted_2(x, axis, by):
    peers = lax.axis_size(axis)
    return lax.ppermute(x, axis, [(i, (i + by) % peers) for i in range(peers)])


def attend(query_rows, key_block_rows, value_block_rows, image_ids):
    row_count, col_count = query_rows.shape
    inverse_root = 1.0 / math.sqrt(HD)
    head_count = col_count // HD
    query_heads = query_rows.reshape(row_count, head_count, HD)
    key_heads = key_block_rows.reshape(row_count, head_count, HD)
    value_heads = value_block_rows.reshape(row_count, head_count, HD)
    scores = (
        jnp.einsum("qhd,khd->hqk", query_heads, key_heads, preferred_element_type=jnp.float32)
        * inverse_root
    )
    allowed = (image_ids[:, None] == image_ids[None, :])[None]
    scores = jnp.where(allowed, scores, -jnp.inf)
    row_top = jnp.max(scores, axis=-1, keepdims=True)
    shifted = jnp.exp(scores - row_top)
    weights = shifted / jnp.sum(shifted, axis=-1, keepdims=True)
    probabilities = weights.astype(jnp.bfloat16)
    live_heads = (image_ids >= 0).astype(jnp.float32)[:, None, None]
    attended = jnp.einsum(
        "hqk,khd->qhd", probabilities, value_heads, preferred_element_type=jnp.float32
    )
    attended = (attended * live_heads).astype(jnp.bfloat16).reshape(row_count, col_count)
    return (weights, probabilities, attended)


def attend_back(query_rows, key_block_rows, value_block_rows, weights, probabilities, grad_live):
    row_count, col_count = query_rows.shape
    inverse_root = 1.0 / math.sqrt(HD)
    head_count = col_count // HD
    query_heads = query_rows.reshape(row_count, head_count, HD)
    key_heads = key_block_rows.reshape(row_count, head_count, HD)
    value_heads = value_block_rows.reshape(row_count, head_count, HD)
    grad_heads = grad_live.reshape(row_count, head_count, HD)
    grad_value = jnp.einsum(
        "hqk,qhd->khd", probabilities, grad_heads, preferred_element_type=jnp.float32
    )
    grad_probs = jnp.einsum(
        "qhd,khd->hqk", grad_heads, value_heads, preferred_element_type=jnp.float32
    )
    row_sums = jnp.sum(weights * grad_probs, axis=-1, keepdims=True)
    grad_scores = (weights * (grad_probs - row_sums) * inverse_root).astype(jnp.bfloat16)
    grad_query = jnp.einsum(
        "hqk,khd->qhd", grad_scores, key_heads, preferred_element_type=jnp.float32
    )
    grad_key = jnp.einsum(
        "hqk,qhd->khd", grad_scores, query_heads, preferred_element_type=jnp.float32
    )
    shape_rows = (row_count, col_count)
    return (
        grad_query.astype(jnp.bfloat16).reshape(shape_rows),
        grad_key.astype(jnp.bfloat16).reshape(shape_rows),
        grad_value.astype(jnp.bfloat16).reshape(shape_rows),
    )


def on_device(queries, key_rows, value_rows, segments, send_block, out_weight, grad_attended):
    half_way = lax.axis_size("dp") // 2
    pad_id = lax.axis_size("dp") * NB
    own_index = lax.axis_index("dp")
    order_keys = jnp.where(send_block > 0, 0, 1).astype(jnp.int32)
    marked = jnp.argsort(order_keys, stable=True)[:MOVE]
    local_ids = jnp.where(segments < pad_id, segments - own_index * NB, -1)

    def outgoing(source):
        return source.reshape((NB, BLOCK) + source.shape[1:])[marked]

    def placed(source, incoming):
        blocks = source.reshape((NB, BLOCK) + source.shape[1:])
        return blocks.at[marked].set(incoming).reshape(source.shape)

    wide_ids = local_ids.astype(jnp.bfloat16)
    arrived = shifted_2(
        (outgoing(queries), outgoing(key_rows), outgoing(value_rows), outgoing(wide_ids)),
        "dp",
        half_way,
    )
    bal_query = placed(queries, arrived[0])
    bal_key = placed(key_rows, arrived[1])
    bal_value = placed(value_rows, arrived[2])
    incoming_ids = arrived[3].astype(jnp.int32)
    incoming_ids = jnp.where(incoming_ids >= 0, incoming_ids + NB, -1)
    bal_ids = placed(local_ids, incoming_ids)
    weights, probabilities, attended = attend(bal_query, bal_key, bal_value, bal_ids)
    partial_value = jnp.dot(attended, out_weight, preferred_element_type=jnp.float32)
    layer_out = lax.psum_scatter(
        partial_value.astype(jnp.bfloat16), "fsdp", scatter_dimension=1, tiled=True
    )
    live_rows = (bal_ids >= 0).astype(jnp.bfloat16)[:, None]
    grad_live = grad_attended * live_rows
    grad_query, grad_key, grad_value = attend_back(
        bal_query, bal_key, bal_value, weights, probabilities, grad_live
    )
    returned = shifted_2(
        (outgoing(grad_query), outgoing(grad_key), outgoing(grad_value)), "dp", half_way
    )
    return (
        layer_out,
        placed(grad_query, returned[0]),
        placed(grad_key, returned[1]),
        placed(grad_value, returned[2]),
    )


def solution(mesh):
    placed = (
        P("dp", "fsdp"),
        P("dp", "fsdp"),
        P("dp", "fsdp"),
        P("dp"),
        P("dp"),
        P("fsdp", None),
        P("dp", "fsdp"),
    )
    return jax.shard_map(
        on_device,
        mesh=mesh,
        in_specs=placed,
        out_specs=(P("dp", "fsdp"), P("dp", "fsdp"), P("dp", "fsdp"), P("dp", "fsdp")),
        check_vma=False,
    )
```

profile of v0, /device:TPU:1, one launch (start us, length us, event | category | flops | bytes accessed | tf_op | source)
XLA Modules:
  0.0 233.2 jit_solution(880086271072954408)
XLA Ops:
  7.2 1.0 copy.79
  8.2 1.0 copy.80
  9.2 1.0 copy.81
  10.2 0.7 compare_select_fusion.2
  10.9 0.7 sort.17
  11.6 0.6 gather_fusion.2
  12.2 5.0 %collective-permute-start.2 = (bf16[2,128,384]{2,1,0:T(8,128)(2,1)S(1)}, bf16[2,128,384]{2,1,0:T(8,128)(2,1)S(1)}, u32[]{:S(2)}, u32[]{:S(2)}) collective-permute-start(bf16[2,128,384]{2,1,0:T(8,128)(2,1)S(1)} %gather_fusion.2), channel_id=1, source_target_pairs={{0,384},{8,392},{16,400},{24,408},{32,416},{40,424},{48,432},{56,4... | collective-permute-start | bytes 589832 | tf_op jit(solution)/shard_map/ppermute | solution.py:16
  17.3 0.7 fusion.37
  18.0 0.6 gather_fusion.1
  18.5 1.9 collective-permute-start.1
  20.5 0.6 gather_fusion.3
  21.1 4.3 %collective-permute-start.3 = (bf16[2,128,384]{2,1,0:T(8,128)(2,1)S(1)}, bf16[2,128,384]{2,1,0:T(8,128)(2,1)S(1)}, u32[]{:S(2)}, u32[]{:S(2)}) collective-permute-start(bf16[2,128,384]{2,1,0:T(8,128)(2,1)S(1)} %gather_fusion.3), channel_id=1, source_target_pairs={{0,384},{8,392},{16,400},{24,408},{32,416},{40,424},{48,432},{56,4... | collective-permute-start | bytes 589832 | tf_op jit(solution)/shard_map/ppermute | solution.py:16
  25.3 0.6 gather_fusion
  25.9 1.9 collective-permute-start
  27.9 0.6 scatter_custom_fusion.1
  28.7 0.6 scatter_fusion.1
  29.4 0.2 copy.44
  29.8 8.2 %collective-permute-done.3 = bf16[2,128,384]{2,1,0:T(8,128)(2,1)S(1)} collective-permute-done((bf16[2,128,384]{2,1,0:T(8,128)(2,1)S(1)}, bf16[2,128,384]{2,1,0:T(8,128)(2,1)S(1)}, u32[]{:S(2)}, u32[]{:S(2)}) %collective-permute-start.3) | collective-permute-done | bytes 196640 | tf_op jit(solution)/shard_map/ppermute | solution.py:16
  38.0 0.6 scatter_fusion.2
  39.0 3.1 %collective-permute-done = bf16[2,128,384]{2,1,0:T(8,128)(2,1)S(1)} collective-permute-done((bf16[2,128,384]{2,1,0:T(8,128)(2,1)S(1)}, bf16[2,128,384]{2,1,0:T(8,128)(2,1)S(1)}, u32[]{:S(2)}, u32[]{:S(2)}) %collective-permute-start) | collective-permute-done | bytes 196640 | tf_op jit(solution)/shard_map/ppermute | solution.py:16
  42.2 0.6 scatter_fusion
  43.3 3.0 %fusion.49 = (f32[3,512]{1,0:T(4,128)S(1)}, f32[3,512,512]{1,2,0:T(8,128)}) fusion(pred[512,512]{0,1:T(8,128)(4,1)S(1)} %broadcast_compare_fusion, bf16[512,3,128]{0,2,1:T(8,128)(2,1)S(1)} %reshape_reshape.25, bf16[512,3,128]{0,2,1:T(8,128)(2,1)S(1)} %reshape_reshape.26), kind=kOutput, calls=%fused_computation.65 | convolution fusion | flops 204472832 | bytes 4200448 | tf_op jit(solution)/shard_map/sub | solution.py:33
  46.3 2.4 %fusion.23 = bf16[3,128,512]{2,1,0:T(8,128)(2,1)S(1)} fusion(bf16[512,3,128]{0,2,1:T(8,128)(2,1)S(1)} %reshape_reshape.24, f32[512]{0:T(512)S(1)} %convert_element_type.56, f32[3,512,512]{1,2,0:T(8,128)} %get-tuple-element.11, f32[3,512]{1,0:T(4,128)S(1)} %get-tuple-element.10), kind=kOutput, calls=%fused_computation.35 | convolution fusion | flops 203292672 | bytes 3940352 | tf_op jit(solution)/shard_map/hqk,khd->qhd/dot_general | solution.py:37
  48.8 0.7 slice-done.1
  49.4 5.4 %convolution_convert_fusion = bf16[512,6144]{1,0:T(8,128)(2,1)} fusion(bf16[512,384]{0,1:T(8,128)(2,1)S(1)} %bitcast.60, bf16[384,6144]{1,0:T(8,128)(2,1)S(1)} %bitcast.48), kind=kOutput, calls=%fused_computation.16 | convolution fusion | flops 2419064832 | bytes 11403264 | tf_op jit(solution)/shard_map/dot_general | solution.py:102
  54.8 1.0 copy-done.4
  56.0 0.7 copy-done.3
  56.8 2.5 %fusion.24 = bf16[512,3,128]{0,2,1:T(8,128)(2,1)S(1)} fusion(bf16[512,3,128]{0,2,1:T(8,128)(2,1)S(1)} %bitcast.58, f32[3,512,512]{1,2,0:T(8,128)} %get-tuple-element.11, f32[3,512]{1,0:T(4,128)S(1)} %get-tuple-element.10), kind=kOutput, calls=%fused_computation.36 | convolution fusion | flops 203096064 | bytes 3938304 | tf_op jit(solution)/shard_map/hqk,qhd->khd/dot_general | solution.py:52
  59.4 0.3 copy.60
  59.7 1.2 gather_fusion.6
  61.0 1.9 collective-permute-start.6
  62.9 1.7 fusion.50
  64.6 5.0 %fusion.25 = bf16[512,3,128]{0,2,1:T(8,128)(2,1)} fusion(bf16[512,3,128]{0,2,1:T(8,128)(2,1)} %copy-done.5, f32[3,512,512]{1,2,0:T(8,128)S(1)} %fusion.50, f32[3,512,512]{1,2,0:T(8,128)} %get-tuple-element.11, f32[3,512]{1,0:T(4,128)S(1)} %get-tuple-element.10), kind=kOutput, calls=%fused_computation.37 | convolution fusion | flops 207030272 | bytes 7084032 | tf_op jit(solution)/shard_map/hqk,qhd->khd/dot_general | solution.py:63
  69.6 1.8 reshape_reshape.28
  71.5 2.0 copy.57
  73.4 2.3 gather_fusion.5
  75.7 5.2 %fusion.28 = bf16[512,3,128]{0,2,1:T(8,128)(2,1)} fusion(bf16[512,3,128]{0,2,1:T(8,128)(2,1)} %copy-done.6, f32[3,512,512]{1,2,0:T(8,128)S(1)} %fusion.50, f32[3,512,512]{1,2,0:T(8,128)} %get-tuple-element.11, f32[3,512]{1,0:T(4,128)S(1)} %get-tuple-element.10), kind=kOutput, calls=%fused_computation.38 | convolution fusion | flops 207030272 | bytes 7084032 | tf_op jit(solution)/shard_map/hqk,khd->qhd/dot_general | solution.py:60
  80.8 4.2 %collective-permute-start.5 = (bf16[2,128,384]{2,1,0:T(8,128)(2,1)}, bf16[2,128,384]{2,1,0:T(8,128)(2,1)S(1)}, u32[]{:S(2)}, u32[]{:S(2)}) collective-permute-start(bf16[2,128,384]{2,1,0:T(8,128)(2,1)} %gather_fusion.5), channel_id=1, source_target_pairs={{0,384},{8,392},{16,400},{24,408},{32,416},{40,424},{48,432},{56,4... | collective-permute-start | bytes 589832 | tf_op jit(solution)/shard_map/ppermute | solution.py:16
  85.1 1.1 reshape_reshape.27
  86.2 0.3 copy.54
  86.5 0.6 gather_fusion.4
  87.1 1.9 collective-permute-start.4
  89.0 1.5 scatter_fusion.5
  90.6 40.2 %collective-permute-done.5 = bf16[2,128,384]{2,1,0:T(8,128)(2,1)S(1)} collective-permute-done((bf16[2,128,384]{2,1,0:T(8,128)(2,1)}, bf16[2,128,384]{2,1,0:T(8,128)(2,1)S(1)}, u32[]{:S(2)}, u32[]{:S(2)}) %collective-permute-start.5) | collective-permute-done | bytes 196640 | tf_op jit(solution)/shard_map/ppermute | solution.py:16
  130.8 2.2 scatter_fusion.4
  133.0 2.2 collective-permute-done.4
  135.2 0.6 scatter_fusion.3
  135.9 90.5 %reduce-scatter.2.cloned.1.call-done = bf16[512,768]{1,0:T(8,128)(2,1)} async-done(((bf16[512,6144]{1,0:T(8,128)(2,1)}), bf16[512,768]{1,0:T(8,128)(2,1)}) %reduce-scatter.2.cloned.1.call-update) | async-done | bytes 786448 | tf_op jit(solution)/shard_map/reduce_scatter | solution.py:103
  (35 shorter events, 1.6 us)
Async XLA Ops:
  7.2 219.2 %reduce-scatter.2.cloned.1.call-start = ((), (), s32[]{:S(2)}) async-start(), calls=%async_computation.1 | async-start | bytes 7077888 | tf_op jit(solution)/shard_map/reduce_scatter | solution.py:103
  12.2 16.5 %collective-permute-start.2 = (bf16[2,128,384]{2,1,0:T(8,128)(2,1)S(1)}, bf16[2,128,384]{2,1,0:T(8,128)(2,1)S(1)}, u32[]{:S(2)}, u32[]{:S(2)}) collective-permute-start(bf16[2,128,384]{2,1,0:T(8,128)(2,1)S(1)} %gather_fusion.2), channel_id=1, source_target_pairs={{0,384},{8,392},{16,400},{24,408},{32,416},{40,424},{48,432},{56,4... | collective-permute-start | bytes 589832 | tf_op jit(solution)/shard_map/ppermute | solution.py:16
  18.5 9.3 %collective-permute-start.1 = (bf16[2,128]{1,0:T(2,128)(2,1)S(1)}, bf16[2,128]{1,0:T(2,128)(2,1)S(1)}, u32[]{:S(2)}, u32[]{:S(2)}) collective-permute-start(bf16[2,128]{1,0:T(2,128)(2,1)S(1)} %gather_fusion.1), channel_id=1, source_target_pairs={{0,384},{8,392},{16,400},{24,408},{32,416},{40,424},{48,432},{56,4... | collective-permute-start | bytes 1544 | tf_op jit(solution)/shard_map/ppermute | solution.py:16
  21.1 16.9 %collective-permute-start.3 = (bf16[2,128,384]{2,1,0:T(8,128)(2,1)S(1)}, bf16[2,128,384]{2,1,0:T(8,128)(2,1)S(1)}, u32[]{:S(2)}, u32[]{:S(2)}) collective-permute-start(bf16[2,128,384]{2,1,0:T(8,128)(2,1)S(1)} %gather_fusion.3), channel_id=1, source_target_pairs={{0,384},{8,392},{16,400},{24,408},{32,416},{40,424},{48,432},{56,4... | collective-permute-start | bytes 589832 | tf_op jit(solution)/shard_map/ppermute | solution.py:16
  25.9 16.3 %collective-permute-start = (bf16[2,128,384]{2,1,0:T(8,128)(2,1)S(1)}, bf16[2,128,384]{2,1,0:T(8,128)(2,1)S(1)}, u32[]{:S(2)}, u32[]{:S(2)}) collective-permute-start(bf16[2,128,384]{2,1,0:T(8,128)(2,1)S(1)} %gather_fusion), channel_id=1, source_target_pairs={{0,384},{8,392},{16,400},{24,408},{32,416},{40,424},{48,432},{56,4... | collective-permute-start | bytes 589832 | tf_op jit(solution)/shard_map/ppermute | solution.py:16
  29.8 16.5 %copy-start.5 = (bf16[512,3,128]{0,2,1:T(8,128)(2,1)}, bf16[512,3,128]{0,2,1:T(8,128)(2,1)S(1)}, u32[]{:S(2)}) copy-start(bf16[512,3,128]{0,2,1:T(8,128)(2,1)S(1)} %reshape_reshape.25) | copy-start | bytes 1179652
  39.0 7.3 %copy-start.6 = (bf16[512,3,128]{0,2,1:T(8,128)(2,1)}, bf16[512,3,128]{0,2,1:T(8,128)(2,1)S(1)}, u32[]{:S(2)}) copy-start(bf16[512,3,128]{0,2,1:T(8,128)(2,1)S(1)} %reshape_reshape.26) | copy-start | bytes 1179652
  43.2 5.5 %copy-start.2 = (bf16[512,3,128]{0,2,1:T(8,128)(2,1)}, bf16[512,3,128]{0,2,1:T(8,128)(2,1)S(1)}, u32[]{:S(2)}) copy-start(bf16[512,3,128]{0,2,1:T(8,128)(2,1)S(1)} %reshape_reshape.24) | copy-start | bytes 1179652
  43.3 5.5 %slice-start = ((s8[4718592]{0:T(1024)(128)(4,1)}), s8[524288]{0:T(1024)(128)(4,1)S(1)}, s32[]{:S(2)}) async-start(s8[4718592]{0:T(1024)(128)(4,1)} %bitcast.47), calls=%async_computation.2 | async-start | bytes 1048576
  46.3 3.1 %slice-start.1 = ((s8[4718592]{0:T(1024)(128)(4,1)}), s8[4194304]{0:T(1024)(128)(4,1)S(1)}, s32[]{:S(2)}) async-start(s8[4718592]{0:T(1024)(128)(4,1)} %bitcast.47), calls=%async_computation.3 | async-start | bytes 8388608
  54.8 1.0 copy-start.4
  56.0 0.7 copy-start.3
  61.0 28.0 %collective-permute-start.6 = (bf16[2,128,384]{2,1,0:T(8,128)(2,1)}, bf16[2,128,384]{2,1,0:T(8,128)(2,1)}, u32[]{:S(2)}, u32[]{:S(2)}) collective-permute-start(bf16[2,128,384]{2,1,0:T(8,128)(2,1)} %gather_fusion.6), channel_id=1, source_target_pairs={{0,384},{8,392},{16,400},{24,408},{32,416},{40,424},{48,432},{56,4... | collective-permute-start | bytes 589832 | tf_op jit(solution)/shard_map/ppermute | solution.py:16
  80.8 50.0 %collective-permute-start.5 = (bf16[2,128,384]{2,1,0:T(8,128)(2,1)}, bf16[2,128,384]{2,1,0:T(8,128)(2,1)S(1)}, u32[]{:S(2)}, u32[]{:S(2)}) collective-permute-start(bf16[2,128,384]{2,1,0:T(8,128)(2,1)} %gather_fusion.5), channel_id=1, source_target_pairs={{0,384},{8,392},{16,400},{24,408},{32,416},{40,424},{48,432},{56,4... | collective-permute-start | bytes 589832 | tf_op jit(solution)/shard_map/ppermute | solution.py:16
  87.1 48.1 %collective-permute-start.4 = (bf16[2,128,384]{2,1,0:T(8,128)(2,1)S(1)}, bf16[2,128,384]{2,1,0:T(8,128)(2,1)S(1)}, u32[]{:S(2)}, u32[]{:S(2)}) collective-permute-start(bf16[2,128,384]{2,1,0:T(8,128)(2,1)S(1)} %gather_fusion.4), channel_id=1, source_target_pairs={{0,384},{8,392},{16,400},{24,408},{32,416},{40,424},{48,432},{56,4... | collective-permute-start | bytes 589832 | tf_op jit(solution)/shard_map/ppermute | solution.py:16
  90.6 135.8 %copy-start = (bf16[4,128,384]{2,1,0:T(8,128)(2,1)}, bf16[4,128,384]{2,1,0:T(8,128)(2,1)S(1)}, u32[]{:S(2)}) copy-start(bf16[4,128,384]{2,1,0:T(8,128)(2,1)S(1)} %scatter_fusion.5) | copy-start | bytes 1179652
  135.9 90.5 %copy-start.1 = (bf16[4,128,384]{2,1,0:T(8,128)(2,1)}, bf16[4,128,384]{2,1,0:T(8,128)(2,1)S(1)}, u32[]{:S(2)}) copy-start(bf16[4,128,384]{2,1,0:T(8,128)(2,1)S(1)} %scatter_fusion.3) | copy-start | bytes 1179652
Sparse Core Ops, SparseCore 0:
  54.9 171.4 reduce-scatter.1
where the time goes:
time: 237 us; the launch traced here: 233 us
  waiting for transfers between devices  144 us (61%)
  matrix products  25.3 us (11%)
  local copies, waits for them, and re-layouts  25.1 us (11%)
  starting transfers between devices  21.3 us (9%)
  between operations  14.4 us (6%)
  other arithmetic  2.94 us (1%)
    reduce_scatter x1, waiting for transfers between devices, on_device(): lax.psum_scatter(partial_value.astype(jnp.bfloat16), 'fsdp', scatter_dime...  90.5 us
    ppermute x7, waiting for transfers between devices, shifted_2(): return lax.ppermute(x, axis, [(i, (i + by) % peers) for i in range(peers)])  53.8 us
    ppermute x7, starting transfers between devices, shifted_2(): return lax.ppermute(x, axis, [(i, (i + by) % peers) for i in range(peers)])  21.2 us
    scatter x9, local copies, waits for them, and re-layouts, placed(): return blocks.at[marked].set(incoming).reshape(source.shape)  7.02 us
    gather x7, local copies, waits for them, and re-layouts, outgoing(): return source.reshape((NB, BLOCK) + source.shape[1:])[marked]  6.43 us
    unnamed x22, local copies, waits for them, and re-layouts  5.59 us
    another operation x6, local copies, waits for them, and re-layouts, placed(): blocks = source.reshape((NB, BLOCK) + source.shape[1:])  5.56 us
    dot_general x1, matrix products, on_device(): jnp.dot(attended, out_weight, preferred_element_type=jnp.float32)  5.36 us
  transfers between devices with their start and end apart: 8, of which 5 were waited for; matrix products, arithmetic and copies ran while one was open for 15% of the time, Pallas kernels for 0%

commit v1 on v0

v1 whole, which is shorter than its diff:
```python
import functools
import math

import jax
import jax.numpy as jnp
from jax import lax
from jax.experimental import pallas as pl
from jax.experimental.pallas import tpu as pltpu
from jax.sharding import PartitionSpec as P

HD = 128
BLOCK = 128
NB = 4
PAIR = 2 * BLOCK
NX = 4
NYL = 4
MESH = pl.DeviceIdType.MESH
BF16 = jnp.bfloat16
F32 = jnp.float32


def marked_and_kept(flags):
    def two(bits):
        first = jnp.where(bits[0] > 0, 0, jnp.where(bits[1] > 0, 1, 2))
        last = jnp.where(bits[3] > 0, 3, jnp.where(bits[2] > 0, 2, 1))
        return first, last

    on = [jnp.where(flag > 0, 1, 0) for flag in flags]
    return two(on), two([1 - bit for bit in on])


def main_kernel(
    nz,
    send_ref,
    seg_ref,
    q_hbm,
    k_hbm,
    v_hbm,
    w_hbm,
    g_hbm,
    out_hbm,
    dq_hbm,
    dk_hbm,
    dv_hbm,
    q_in,
    k_in,
    v_in,
    g_in,
    qp,
    kp,
    vp,
    gp,
    seg_col,
    weights,
    probs,
    dscore,
    moved_out,
    grad_out,
    grad_arrived,
    relay_kept,
    rows_all,
    w_all,
    acc,
    packed_out,
    dq_out,
    dk_out,
    dv_out,
    load_sem,
    store_sem,
    y_send,
    y_recv,
    x_send,
    x_recv,
    f_send,
    f_recv,
    z_send,
    z_recv,
    s_send,
    s_recv,
):
    width = q_hbm.shape[1]
    heads = width // HD
    cols = w_all.shape[2]
    piece = width // (nz * 2)
    half = nz // 2
    inverse_root = 1.0 / math.sqrt(HD)

    g = lax.axis_index("dp")
    f = lax.axis_index("fsdp")
    per_y = nz * 2
    n_dp = NYL * per_y
    pad_id = n_dp * NB
    yl = g // per_y
    z = (g % per_y) // 2
    c = g % 2
    x = f % NX
    yh = f // NX

    def dev(dp, fsdp):
        return {"dp": dp, "fsdp": fsdp}

    partner = (g + n_dp // 2) % n_dp
    p0 = dev(partner, f)
    p1 = dev(partner, (f + NX) % (2 * NX))
    xs = [dev(g, yh * NX + (x + d) % NX) for d in range(NX)]
    right, left = xs[1], xs[3]
    z_right = dev(yl * per_y + ((z + 1) % nz) * 2 + c, f)
    z_left = dev(yl * per_y + ((z + nz - 1) % nz) * 2 + c, f)
    sibling = dev(g + 1 - 2 * c, f)
    mirror_dp = (NYL - 1 - yl) * per_y + z * 2 + c
    mirrors = [dev(mirror_dp, (1 - yh) * NX + (x + d) % NX) for d in range(NX)]
    others = [p0, p1, xs[1], xs[2], xs[3], z_right, z_left, sibling] + mirrors

    barrier = pltpu.get_barrier_semaphore()
    for other in others:
        pl.semaphore_signal(barrier, inc=1, device_id=other, device_id_type=MESH)

    my_cols = pl.ds(pl.multiple_of(f * cols, 128), cols)
    loads = [
        pltpu.make_async_copy(src, dst, load_sem.at[i])
        for i, (src, dst) in enumerate(
            [
                (q_hbm, q_in),
                (k_hbm, k_in),
                (v_hbm, v_in),
                (g_hbm, g_in),
                (w_hbm.at[:, my_cols], w_all.at[0]),
            ]
        )
    ]
    for load in loads:
        load.start()

    on = [send_ref[t].astype(F32) for t in range(NB)]
    off = [1.0 - flag for flag in on]

    def first_and_second(is_set, is_clear):
        return [
            [(0, is_set[0]), (1, is_clear[0] * is_set[1]), (2, is_clear[0] * is_clear[1])],
            [(3, is_set[3]), (2, is_clear[3] * is_set[2]), (1, is_clear[3] * is_clear[2])],
        ]

    order = first_and_second(off, on) + first_and_second(on, off)

    def pick(source, i):
        total = None
        for t, factor in order[i]:
            block = source(t)
            part = block * jnp.full(block.shape, factor, F32).astype(block.dtype)
            total = part if total is None else total + part
        return total

    def pick_block(ref, i):
        return pick(lambda t: ref[pl.ds(t * BLOCK, BLOCK), :], i)

    sends = []

    def remote(src, dst, ssem, rsem, device):
        copy = pltpu.make_async_remote_copy(
            src_ref=src, dst_ref=dst, send_sem=ssem, recv_sem=rsem, device_id=device, device_id_type=MESH
        )
        return copy

    def go(copy):
        copy.start()
        sends.append(copy)

    seg_rows = []
    for i in range(NB):
        row = pick(lambda t: seg_ref[pl.ds(t, 1), :].astype(F32), i)
        seg_rows.append(row)
        seg_col[i] = jnp.transpose(jnp.broadcast_to(row, (BLOCK, BLOCK)))

    def pack(src, dst, first):
        for i in range(first, first + 2):
            dst[pl.ds(i * BLOCK, BLOCK), :] = pick_block(src, i)

    def forward(pair):
        base = pair * PAIR
        for i in range(2):
            col = seg_col[pair * 2 + i]
            live = jnp.where(col < float(pad_id), 1.0, 0.0)
            allowed = jnp.concatenate(
                [col == seg_rows[pair * 2], col == seg_rows[pair * 2 + 1]], axis=1
            )
            for h in range(heads):
                lanes = pl.ds(h * HD, HD)
                q = qp[pl.ds(base + i * BLOCK, BLOCK), lanes]
                k = kp[pl.ds(base, PAIR), lanes]
                v = vp[pl.ds(base, PAIR), lanes]
                scores = (
                    lax.dot_general(q, k, (((1,), (1,)), ((), ())), preferred_element_type=F32)
                    * inverse_root
                )
                scores = jnp.where(allowed, scores, -jnp.inf)
                top = jnp.max(scores, axis=1, keepdims=True)
                raised = jnp.exp(scores - top)
                share = raised * (1.0 / jnp.sum(raised, axis=1, keepdims=True))
                rounded = share.astype(BF16)
                weights[pair * heads + h, pl.ds(i * BLOCK, BLOCK), :] = share
                probs[pair * heads + h, pl.ds(i * BLOCK, BLOCK), :] = rounded
                mixed = jnp.dot(rounded, v, preferred_element_type=F32)
                mixed = (mixed * live).astype(BF16)
                if pair == 1:
                    moved_out[pl.ds(i * BLOCK, BLOCK), lanes] = mixed
                else:
                    rows_all[0, pl.ds(i * BLOCK, BLOCK), lanes] = mixed

    def backward(pair):
        base = pair * PAIR
        for h in range(heads):
            lanes = pl.ds(h * HD, HD)
            tile = pair * heads + h
            q = qp[pl.ds(base, PAIR), lanes]
            k = kp[pl.ds(base, PAIR), lanes]
            v = vp[pl.ds(base, PAIR), lanes]
            for i in range(2):
                rows = pl.ds(i * BLOCK, BLOCK)
                grad = gp[pl.ds(base + i * BLOCK, BLOCK), lanes]
                grad_probs = lax.dot_general(grad, v, (((1,), (1,)), ((), ())), preferred_element_type=F32)
                share = weights[tile, rows, :]
                row_sums = jnp.sum(share * grad_probs, axis=1, keepdims=True)
                grad_scores = (share * (grad_probs - row_sums) * inverse_root).astype(BF16)
                dscore[rows, :] = grad_scores
                dq = jnp.dot(grad_scores, k, preferred_element_type=F32)
                dq_out[pl.ds(base + i * BLOCK, BLOCK), lanes] = dq.astype(BF16)
            grad = gp[pl.ds(base, PAIR), lanes]
            over_rows = (((0,), (0,)), ((), ()))
            dk = lax.dot_general(dscore[...], q, over_rows, preferred_element_type=F32)
            dk_out[pl.ds(base, PAIR), lanes] = dk.astype(BF16)
            dv = lax.dot_general(probs[tile], grad, over_rows, preferred_element_type=F32)
            dv_out[pl.ds(base, PAIR), lanes] = dv.astype(BF16)

    stores = []

    def store_grads(pair):
        rows = pl.ds(pair * PAIR, PAIR)
        for i, (src, dst) in enumerate([(dq_out, dq_hbm), (dk_out, dk_hbm), (dv_out, dv_hbm)]):
            copy = pltpu.make_async_copy(src.at[rows, :], dst.at[rows, :], store_sem.at[pair * 3 + i])
            copy.start()
            stores.append(copy)

    def live_grad(i, block):
        live = jnp.where(seg_col[i] < float(pad_id), 1.0, 0.0).astype(BF16)
        for h in range(heads):
            lanes = pl.ds(h * HD, HD)
            gp[pl.ds(i * BLOCK, BLOCK), lanes] = block[:, h * HD : (h + 1) * HD] * live

    for load in loads[:3]:
        load.wait()
    for src, dst in ((q_in, qp), (k_in, kp), (v_in, vp)):
        pack(src, dst, 2)
    forward(1)

    pl.semaphore_wait(barrier, len(others))

    def piece_rows(at):
        return pl.ds(pl.multiple_of(at * (2 * piece) + c * piece, 16), piece)

    def fetch(slot, device, owner):
        at = pl.ds(pl.multiple_of(owner * cols, 128), cols)
        return remote(
            w_hbm.at[piece_rows(z), at],
            w_all.at[slot, piece_rows(z), :],
            f_send.at[slot],
            f_recv.at[slot],
            device,
        )

    fetches = {}
    for d in (1, 3, 2):
        fetches[NX - d] = fetch(NX - d, xs[d], yh * NX + (x + d) % NX)
    for d in range(NX):
        slot = NX + (NX - d) % NX
        fetches[slot] = fetch(slot, mirrors[d], (1 - yh) * NX + (x + d) % NX)
    for copy in fetches.values():
        go(copy)

    def block_of(ref, slot, b):
        return ref.at[slot, pl.ds(b * BLOCK, BLOCK), :]

    def two_rows(b):
        return pl.ds(b * BLOCK, BLOCK)

    y_copies = [
        remote(moved_out.at[two_rows(0), :], block_of(rows_all, 0, 2), y_send.at[0], y_recv.at[0], p0),
        remote(moved_out.at[two_rows(1), :], block_of(rows_all, 0, 3), y_send.at[1], y_recv.at[1], p0),
        remote(moved_out.at[two_rows(0), :], block_of(rows_all, NX, 2), y_send.at[2], y_recv.at[2], p1),
        remote(moved_out.at[two_rows(1), :], block_of(rows_all, NX, 3), y_send.at[3], y_recv.at[3], p1),
        remote(block_of(rows_all, 0, 0), relay_kept.at[0], y_send.at[4], y_recv.at[4], p0),
        remote(block_of(rows_all, 0, 1), relay_kept.at[1], y_send.at[5], y_recv.at[5], p1),
        remote(relay_kept.at[0], block_of(rows_all, NX, 0), y_send.at[6], y_recv.at[6], p1),
        remote(relay_kept.at[1], block_of(rows_all, NX, 1), y_send.at[7], y_recv.at[7], p0),
        remote(grad_out, grad_arrived, y_send.at[8], y_recv.at[8], p0),
    ]
    for i in (0, 2, 1, 3):
        go(y_copies[i])

    for src, dst in ((q_in, qp), (k_in, kp), (v_in, vp)):
        pack(src, dst, 0)
    forward(0)
    go(y_copies[4])
    go(y_copies[5])

    groups = [(0, 0), (0, 2), (NX, 2), (NX, 0)]
    x_copies = {}
    for n, (slot, first) in enumerate(groups):
        for b in range(2):
            at = first + b
            sem = (n * 2 + b) * 3
            x_copies[n, b, "r"] = remote(
                block_of(rows_all, slot, at),
                block_of(rows_all, slot + 3, at),
                x_send.at[sem],
                x_recv.at[sem],
                right,
            )
            x_copies[n, b, "l"] = remote(
                block_of(rows_all, slot, at),
                block_of(rows_all, slot + 1, at),
                x_send.at[sem + 1],
                x_recv.at[sem + 1],
                left,
            )
            x_copies[n, b, "far"] = remote(
                block_of(rows_all, slot + (3 if b == 0 else 1), at),
                block_of(rows_all, slot + 2, at),
                x_send.at[sem + 2],
                x_recv.at[sem + 2],
                right if b == 0 else left,
            )

    def x_start(n, b):
        go(x_copies[n, b, "r" if b == 0 else "l"])
        go(x_copies[n, b, "l" if b == 0 else "r"])

    def x_relay(n, b):
        x_copies[n, b, "r" if b == 0 else "l"].wait_recv()
        go(x_copies[n, b, "far"])

    def x_finish(n):
        for b in range(2):
            x_copies[n, b, "l" if b == 0 else "r"].wait_recv()
            x_copies[n, b, "far"].wait_recv()

    x_start(0, 0)
    x_start(0, 1)

    loads[3].wait()
    for i in range(2):
        grad_out[pl.ds(i * BLOCK, BLOCK), :] = pick_block(g_in, 2 + i)
    go(y_copies[8])

    subs = [(1, NX), (NX, 2 * NX)]
    last_step = {("r", 0): half - 1, ("r", 1): half - 2, ("l", 0): half - 2, ("l", 1): half - 1}

    def w_piece(sub, at):
        first, end = subs[sub]
        return w_all.at[pl.ds(first, end - first), piece_rows(at), :]

    z_copies = {}
    s_copies = {}
    for sub in range(2):
        s_copies["own", sub, 0] = (sub * nz, z)
        for way in ("r", "l"):
            for s in range(last_step[way, sub] + 1):
                at = (z + nz - s) % nz if way == "r" else (z + s) % nz
                sem = ((0 if way == "r" else 1) * 2 + sub) * half + s
                z_copies[way, sub, s] = remote(
                    w_piece(sub, at),
                    w_piece(sub, at),
                    z_send.at[sem],
                    z_recv.at[sem],
                    z_right if way == "r" else z_left,
                )
                came = (z + nz - s - 1) % nz if way == "r" else (z + s + 1) % nz
                number = 1 + s if way == "r" else half + 1 + s
                if way == "l" and sub == 1:
                    number = half + s
                s_copies[way, sub, s] = (sub * nz + number, came)
    for key, (sem, at) in list(s_copies.items()):
        sub = key[1]
        s_copies[key] = remote(w_piece(sub, at), w_piece(sub, at), s_send.at[sem], s_recv.at[sem], sibling)

    def ring_start(sub):
        first, end = subs[sub]
        for slot in range(first, end):
            fetches[slot].wait_recv()
        for way in ("r", "l"):
            if (way, sub, 0) in z_copies:
                go(z_copies[way, sub, 0])
        go(s_copies["own", sub, 0])

    def ring_step(sub, s):
        for way in ("r", "l"):
            if (way, sub, s) in z_copies:
                z_copies[way, sub, s].wait_recv()
                if (way, sub, s + 1) in z_copies:
                    go(z_copies[way, sub, s + 1])
                go(s_copies[way, sub, s])

    steps = [(sub, s) for s in range(half) for sub in range(2)]

    def ring_steps(count):
        for _ in range(count):
            if steps:
                ring_step(*steps.pop(0))

    def y_arrived(i):
        y_copies[i].wait_recv()

    def project(pair, slots, init):
        rows = pl.ds(pair * PAIR, PAIR)
        for n in range(0, cols, min(cols, 256)):
            lanes = pl.ds(n, min(cols, 256))
            total = None if init else acc[rows, lanes]
            for slot in slots:
                part = jnp.dot(rows_all[slot, rows, :], w_all[slot, :, lanes], preferred_element_type=F32)
                total = part if total is None else total + part
            acc[rows, lanes] = total

    ring_start(0)
    for i in range(2):
        live_grad(i, pick_block(g_in, i))
    backward(0)
    store_grads(0)
    ring_start(1)
    x_relay(0, 0)
    x_relay(0, 1)
    ring_steps(1)
    y_arrived(0)
    x_start(1, 0)
    y_arrived(2)
    x_start(2, 0)
    ring_steps(1)
    y_arrived(1)
    x_start(1, 1)
    y_arrived(3)
    x_start(2, 1)
    y_arrived(4)
    go(y_copies[6])
    y_arrived(5)
    go(y_copies[7])
    loads[4].wait()
    project(0, [0], True)
    project(1, [0], True)
    ring_steps(1)
    x_relay(1, 0)
    x_relay(2, 0)
    ring_steps(1)
    x_relay(1, 1)
    x_relay(2, 1)
    ring_steps(2)
    y_arrived(6)
    x_start(3, 0)
    y_arrived(7)
    x_start(3, 1)
    ring_steps(2)
    x_relay(3, 0)
    x_relay(3, 1)
    ring_steps(1)
    y_arrived(8)
    for i in range(2):
        live_grad(2 + i, grad_arrived[pl.ds(i * BLOCK, BLOCK), :])
    backward(1)
    store_grads(1)
    ring_steps(2 * half)
    for copy in s_copies.values():
        copy.wait_recv()
    x_finish(0)
    project(0, [1, 2, 3], False)
    x_finish(1)
    project(1, [1, 2, 3], False)
    x_finish(2)
    project(1, [4, 5, 6, 7], False)
    packed_out[pl.ds(PAIR, PAIR), :] = acc[pl.ds(PAIR, PAIR), :].astype(BF16)
    late = pltpu.make_async_copy(
        packed_out.at[pl.ds(PAIR, PAIR), :], out_hbm.at[pl.ds(PAIR, PAIR), :], store_sem.at[6]
    )
    late.start()
    x_finish(3)
    project(0, [4, 5, 6, 7], False)
    packed_out[pl.ds(0, PAIR), :] = acc[pl.ds(0, PAIR), :].astype(BF16)
    last = pltpu.make_async_copy(
        packed_out.at[pl.ds(0, PAIR), :], out_hbm.at[pl.ds(0, PAIR), :], store_sem.at[7]
    )
    last.start()
    for copy in sends:
        copy.wait_send()
    for copy in stores + [late, last]:
        copy.wait()


def place_kernel(send_ref, out_p, dq_p, dk_p, dv_p, out, dq, dk, dv, sem):
    (m0, m1), (k0, k1) = marked_and_kept([send_ref[t] for t in range(NB)])
    copies = []
    for i, t in enumerate([k0, k1, m0, m1]):
        to = pl.ds(pl.multiple_of(t * BLOCK, BLOCK), BLOCK)
        for n, (src, dst) in enumerate([(out_p, out), (dq_p, dq), (dk_p, dk), (dv_p, dv)]):
            copies.append(
                pltpu.make_async_copy(src.at[pl.ds(i * BLOCK, BLOCK), :], dst.at[to, :], sem.at[n * NB + i])
            )
    for copy in copies:
        copy.start()
    for copy in copies:
        copy.wait()


def on_device(nz, queries, key_rows, value_rows, segments, send_block, out_weight, grad_attended):
    rows, width = queries.shape
    cols = out_weight.shape[1] // (2 * NX)
    heads = width // HD
    half = nz // 2
    anywhere = pl.BlockSpec(memory_space=pltpu.HBM)
    wide = jax.ShapeDtypeStruct((rows, cols), BF16)
    narrow = jax.ShapeDtypeStruct((rows, width), BF16)
    dma = pltpu.SemaphoreType.DMA
    packed = pl.pallas_call(
        functools.partial(main_kernel, nz),
        out_shape=(wide, narrow, narrow, narrow),
        in_specs=[
            pl.BlockSpec(memory_space=pltpu.SMEM),
            pl.BlockSpec(memory_space=pltpu.VMEM),
        ]
        + [anywhere] * 5,
        out_specs=(anywhere,) * 4,
        scratch_shapes=[pltpu.VMEM((rows, width), BF16)] * 8
        + [
            pltpu.VMEM((NB, BLOCK, BLOCK), F32),
            pltpu.VMEM((2 * heads, PAIR, PAIR), F32),
            pltpu.VMEM((2 * heads, PAIR, PAIR), BF16),
            pltpu.VMEM((PAIR, PAIR), BF16),
            pltpu.VMEM((PAIR, width), BF16),
            pltpu.VMEM((PAIR, width), BF16),
            pltpu.VMEM((PAIR, width), BF16),
            pltpu.VMEM((2, BLOCK, width), BF16),
            pltpu.VMEM((2 * NX, rows, width), BF16),
            pltpu.VMEM((2 * NX, width, cols), BF16),
            pltpu.VMEM((rows, cols), F32),
            pltpu.VMEM((rows, cols), BF16),
        ]
        + [pltpu.VMEM((rows, width), BF16)] * 3
        + [
            dma((5,)),
            dma((8,)),
            dma((9,)),
            dma((9,)),
            dma((24,)),
            dma((24,)),
            dma((8,)),
            dma((8,)),
            dma((4 * half,)),
            dma((4 * half,)),
            dma((2 * nz,)),
            dma((2 * nz,)),
        ],
        compiler_params=pltpu.CompilerParams(
            collective_id=0, has_side_effects=True, vmem_limit_bytes=60 * 1024 * 1024
        ),
        name="attend_gather_project",
    )(
        send_block,
        segments.reshape(NB, BLOCK),
        queries,
        key_rows,
        value_rows,
        out_weight,
        grad_attended,
    )
    return pl.pallas_call(
        place_kernel,
        out_shape=(wide, narrow, narrow, narrow),
        in_specs=[pl.BlockSpec(memory_space=pltpu.SMEM)] + [anywhere] * 4,
        out_specs=(anywhere,) * 4,
        scratch_shapes=[dma((4 * NB,))],
        name="place_blocks",
    )(send_block, *packed)


def solution(mesh):
    nz = mesh.shape["dp"] // (NYL * 2)
    return jax.shard_map(
        functools.partial(on_device, nz),
        mesh=mesh,
        in_specs=(
            P("dp", "fsdp"),
            P("dp", "fsdp"),
            P("dp", "fsdp"),
            P("dp"),
            P("dp"),
            P("fsdp", None),
            P("dp", "fsdp"),
        ),
        out_specs=(P("dp", "fsdp"),) * 4,
        check_vma=False,
    )
```

time: 237 us -> 128 us (0.54)
  waiting for transfers between devices: 144 us -> 0 us
  Pallas kernels: 0 us -> 125 us
  matrix products: 25.3 us -> 0 us
  local copies, waits for them, and re-layouts: 25.1 us -> 0 us
  starting transfers between devices: 21.3 us -> 0 us
  between operations: 14.4 us -> 0.64 us
  other arithmetic: 2.94 us -> 0 us
    pallas_call x0 -> x2, Pallas kernels: none -> 125 us  [the longest x1 63.8 us: on_device(): pl.pallas_call(functools.partial(main_kernel, nz), out_shape=(wide, narro...]
    reduce_scatter x1 -> x0, waiting for transfers between devices: 90.5 us -> none  [on_device(): lax.psum_scatter(partial_value.astype(jnp.bfloat16), 'fsdp', scatter_dime...]
    ppermute x7 -> x0, waiting for transfers between devices: 53.8 us -> none  [shifted_2(): return lax.ppermute(x, axis, [(i, (i + by) % peers) for i in range(peers)])]
    dot_general x6 -> x0, matrix products: 22.2 us -> none  [the longest x1 5.36 us: on_device(): jnp.dot(attended, out_weight, preferred_element_type=jnp.float32)]
    ppermute x7 -> x0, starting transfers between devices: 21.2 us -> none  [shifted_2(): return lax.ppermute(x, axis, [(i, (i + by) % peers) for i in range(peers)])]
    scatter x9 -> x0, local copies, waits for them, and re-layouts: 7.02 us -> none  [placed(): return blocks.at[marked].set(incoming).reshape(source.shape)]
    gather x7 -> x0, local copies, waits for them, and re-layouts: 6.43 us -> none  [outgoing(): return source.reshape((NB, BLOCK) + source.shape[1:])[marked]]
    another operation x9 -> x0, local copies, waits for them, and re-layouts: 6.02 us -> none  [the longest x6 5.56 us: placed(): blocks = source.reshape((NB, BLOCK) + source.shape[1:])]
  transfers between devices with their start and end apart: 8 -> 0, of which waited for: 5 -> 0; matrix products, arithmetic and copies ran while one was open for 15% -> 0% of each run, Pallas kernels for 0% -> 0%
where the time goes in v1:
time: 128 us; the launch traced here: 126 us
  Pallas kernels  125 us (98%)
    pallas_call x1, Pallas kernels, on_device(): pl.pallas_call(functools.partial(main_kernel, nz), out_shape=(wide, narro...  63.8 us
    pallas_call x1, Pallas kernels, on_device(): pl.pallas_call(place_kernel, out_shape=(wide, narrow, narrow, narrow), in...  61.5 us

profile of v1, /device:TPU:1, one launch (start us, length us, event | category | flops | bytes accessed | tf_op | source)
XLA Modules:
  0.0 125.9 jit_solution(3888294570727728132)
XLA Ops:
  0.6 63.8 %attend_gather_project.1 = (bf16[512,768]{1,0:T(8,128)(2,1)}, bf16[512,384]{1,0:T(8,128)(2,1)}, bf16[512,384]{1,0:T(8,128)(2,1)}, bf16[512,384]{1,0:T(8,128)(2,1)}) custom-call(s32[4]{0:T(128)} %send_ref.3, s32[4,128]{1,0:T(4,128)} %bitcast.1, bf16[512,384]{1,0:T(8,128)(2,1)} %q_hbm.1, bf16[512,384]{1,0:T(8,128)(2,1)} %k_hbm.1, bf16[512,384]{1,0:T(8,128)(2,1)} %v_hbm.1, ...), custom_call_target="tpu_custom_call" | custom-call | tf_op jit(solution)/shard_map/attend_gather_project/pallas_call | solution.py:518
  64.4 61.5 %place_blocks.1 = (bf16[512,768]{1,0:T(8,128)(2,1)}, bf16[512,384]{1,0:T(8,128)(2,1)}, bf16[512,384]{1,0:T(8,128)(2,1)}, bf16[512,384]{1,0:T(8,128)(2,1)}) custom-call(s32[4]{0:T(128)} %send_ref.3, bf16[512,768]{1,0:T(8,128)(2,1)} %get-tuple-element.8.out_p, bf16[512,384]{1,0:T(8,128)(2,1)} %get-tuple-element.9.dq_p, ...), custom_call_target="tpu_custom_call" | custom-call | tf_op jit(solution)/shard_map/place_blocks/pallas_call | solution.py:570

commit v2 on v1

--- a/solution.py
+++ b/solution.py
@@ -246,12 +246,6 @@
             lanes = pl.ds(h * HD, HD)
             gp[pl.ds(i * BLOCK, BLOCK), lanes] = block[:, h * HD : (h + 1) * HD] * live
 
-    for load in loads[:3]:
-        load.wait()
-    for src, dst in ((q_in, qp), (k_in, kp), (v_in, vp)):
-        pack(src, dst, 2)
-    forward(1)
-
     pl.semaphore_wait(barrier, len(others))
 
     def piece_rows(at):
@@ -273,8 +267,14 @@
     for d in range(NX):
         slot = NX + (NX - d) % NX
         fetches[slot] = fetch(slot, mirrors[d], (1 - yh) * NX + (x + d) % NX)
-    for copy in fetches.values():
-        go(copy)
+    for slot in list(range(NX, 2 * NX)) + list(range(1, NX)):
+        go(fetches[slot])
+
+    for load in loads[:3]:
+        load.wait()
+    for src, dst in ((q_in, qp), (k_in, kp), (v_in, vp)):
+        pack(src, dst, 2)
+    forward(1)
 
     def block_of(ref, slot, b):
         return ref.at[slot, pl.ds(b * BLOCK, BLOCK), :]
@@ -291,10 +291,15 @@
         remote(block_of(rows_all, 0, 1), relay_kept.at[1], y_send.at[5], y_recv.at[5], p1),
         remote(relay_kept.at[0], block_of(rows_all, NX, 0), y_send.at[6], y_recv.at[6], p1),
         remote(relay_kept.at[1], block_of(rows_all, NX, 1), y_send.at[7], y_recv.at[7], p0),
-        remote(grad_out, grad_arrived, y_send.at[8], y_recv.at[8], p0),
+        remote(grad_out.at[two_rows(0), :], grad_arrived.at[two_rows(0), :], y_send.at[8], y_recv.at[8], p0),
+        remote(grad_out.at[two_rows(1), :], grad_arrived.at[two_rows(1), :], y_send.at[9], y_recv.at[9], p0),
     ]
     for i in (0, 2, 1, 3):
         go(y_copies[i])
+    loads[3].wait()
+    for i in range(2):
+        grad_out[pl.ds(i * BLOCK, BLOCK), :] = pick_block(g_in, 2 + i)
+    go(y_copies[8])
 
     for src, dst in ((q_in, qp), (k_in, kp), (v_in, vp)):
         pack(src, dst, 0)
@@ -346,11 +351,6 @@
     x_start(0, 0)
     x_start(0, 1)
 
-    loads[3].wait()
-    for i in range(2):
-        grad_out[pl.ds(i * BLOCK, BLOCK), :] = pick_block(g_in, 2 + i)
-    go(y_copies[8])
-
     subs = [(1, NX), (NX, 2 * NX)]
     last_step = {("r", 0): half - 1, ("r", 1): half - 2, ("l", 0): half - 2, ("l", 1): half - 1}
 
@@ -432,24 +432,25 @@
     x_start(1, 0)
     y_arrived(2)
     x_start(2, 0)
-    ring_steps(1)
+    ring_steps(2)
+    x_relay(1, 0)
+    x_relay(2, 0)
     y_arrived(1)
     x_start(1, 1)
     y_arrived(3)
     x_start(2, 1)
+    ring_steps(2)
+    x_relay(1, 1)
+    x_relay(2, 1)
+    ring_steps(1)
     y_arrived(4)
     go(y_copies[6])
     y_arrived(5)
     go(y_copies[7])
+    go(y_copies[9])
     loads[4].wait()
     project(0, [0], True)
     project(1, [0], True)
-    ring_steps(1)
-    x_relay(1, 0)
-    x_relay(2, 0)
-    ring_steps(1)
-    x_relay(1, 1)
-    x_relay(2, 1)
     ring_steps(2)
     y_arrived(6)
     x_start(3, 0)
@@ -460,6 +461,7 @@
     x_relay(3, 1)
     ring_steps(1)
     y_arrived(8)
+    y_arrived(9)
     for i in range(2):
         live_grad(2 + i, grad_arrived[pl.ds(i * BLOCK, BLOCK), :])
     backward(1)
@@ -543,8 +545,8 @@
         + [
             dma((5,)),
             dma((8,)),
-            dma((9,)),
-            dma((9,)),
+            dma((10,)),
+            dma((10,)),
             dma((24,)),
             dma((24,)),
             dma((8,)),
@@ -570,7 +572,7 @@
     return pl.pallas_call(
         place_kernel,
         out_shape=(wide, narrow, narrow, narrow),
-        in_specs=[pl.BlockSpec(memory_space=pltpu.SMEM)] + [anywhere] * 4,
+        in_specs=[pl.BlockSpec(memory_space=pltpu.SMEM)] + [pl.BlockSpec(memory_space=pltpu.VMEM)] * 4,
         out_specs=(anywhere,) * 4,
         scratch_shapes=[dma((4 * NB,))],
         name="place_blocks",

time: 128 us -> 66.6 us (0.52); the launches traced: 126 us -> 66.4 us
  Pallas kernels: 125 us -> 65.7 us
    pallas_call x1, Pallas kernels: 61.5 us -> 2.89 us  [on_device(): pl.pallas_call(place_kernel, out_shape=(wide, narrow, narrow, narrow), in...]
where the time goes in v2:
time: 66.6 us; the launch traced here: 66.4 us
  Pallas kernels  65.7 us (99%)
    pallas_call x1, Pallas kernels, on_device(): pl.pallas_call(functools.partial(main_kernel, nz), out_shape=(wide, narro...  62.8 us
    pallas_call x1, Pallas kernels, on_device(): pl.pallas_call(place_kernel, out_shape=(wide, narrow, narrow, narrow), in...  2.89 us

profile of v2, /device:TPU:1, one launch (start us, length us, event | category | flops | bytes accessed | tf_op | source)
XLA Modules:
  0.0 66.4 jit_solution(2232372268162744444)
XLA Ops:
  0.6 62.8 %attend_gather_project.1 = (bf16[512,768]{1,0:T(8,128)(2,1)}, bf16[512,384]{1,0:T(8,128)(2,1)}, bf16[512,384]{1,0:T(8,128)(2,1)}, bf16[512,384]{1,0:T(8,128)(2,1)}) custom-call(s32[4]{0:T(128)} %send_ref.3, s32[4,128]{1,0:T(4,128)} %bitcast.1, bf16[512,384]{1,0:T(8,128)(2,1)} %q_hbm.1, bf16[512,384]{1,0:T(8,128)(2,1)} %k_hbm.1, bf16[512,384]{1,0:T(8,128)(2,1)} %v_hbm.1, ...), custom_call_target="tpu_custom_call" | custom-call | tf_op jit(solution)/shard_map/attend_gather_project/pallas_call | solution.py:520
  63.5 2.9 %place_blocks.1 = (bf16[512,768]{1,0:T(8,128)(2,1)}, bf16[512,384]{1,0:T(8,128)(2,1)}, bf16[512,384]{1,0:T(8,128)(2,1)}, bf16[512,384]{1,0:T(8,128)(2,1)}) custom-call(s32[4]{0:T(128)} %send_ref.3, bf16[512,768]{1,0:T(8,128)(2,1)} %get-tuple-element.8.out_p, bf16[512,384]{1,0:T(8,128)(2,1)} %get-tuple-element.9.dq_p, ...), custom_call_target="tpu_custom_call" | custom-call | tf_op jit(solution)/shard_map/place_blocks/pallas_call | solution.py:572

commit v3 on v2

--- a/solution.py
+++ b/solution.py
@@ -206,9 +206,9 @@
                 else:
                     rows_all[0, pl.ds(i * BLOCK, BLOCK), lanes] = mixed
 
-    def backward(pair):
+    def backward(pair, some):
         base = pair * PAIR
-        for h in range(heads):
+        for h in some:
             lanes = pl.ds(h * HD, HD)
             tile = pair * heads + h
             q = qp[pl.ds(base, PAIR), lanes]
@@ -251,24 +251,24 @@
     def piece_rows(at):
         return pl.ds(pl.multiple_of(at * (2 * piece) + c * piece, 16), piece)
 
-    def fetch(slot, device, owner):
-        at = pl.ds(pl.multiple_of(owner * cols, 128), cols)
-        return remote(
-            w_hbm.at[piece_rows(z), at],
-            w_all.at[slot, piece_rows(z), :],
-            f_send.at[slot],
-            f_recv.at[slot],
-            device,
-        )
-
     fetches = {}
-    for d in (1, 3, 2):
-        fetches[NX - d] = fetch(NX - d, xs[d], yh * NX + (x + d) % NX)
-    for d in range(NX):
-        slot = NX + (NX - d) % NX
-        fetches[slot] = fetch(slot, mirrors[d], (1 - yh) * NX + (x + d) % NX)
-    for slot in list(range(NX, 2 * NX)) + list(range(1, NX)):
-        go(fetches[slot])
+    for way, piece_at in (("near", z), ("far", (z + half) % nz)):
+        for d in range(2 * NX):
+            if d == 0:
+                continue
+            slot = NX - d if d < NX else NX + (2 * NX - d) % NX
+            owner = (yh if d < NX else 1 - yh) * NX + (x + d) % NX
+            sem = slot + (2 * NX if way == "far" else 0)
+            fetches[way, slot] = remote(
+                w_hbm.at[piece_rows(piece_at), pl.ds(pl.multiple_of(owner * cols, 128), cols)],
+                w_all.at[slot, piece_rows(piece_at), :],
+                f_send.at[sem],
+                f_recv.at[sem],
+                xs[d] if d < NX else mirrors[d - NX],
+            )
+    fetch_order = list(range(NX, 2 * NX)) + list(range(1, NX))
+    for slot in fetch_order:
+        go(fetches["near", slot])
 
     for load in loads[:3]:
         load.wait()
@@ -296,10 +296,6 @@
     ]
     for i in (0, 2, 1, 3):
         go(y_copies[i])
-    loads[3].wait()
-    for i in range(2):
-        grad_out[pl.ds(i * BLOCK, BLOCK), :] = pick_block(g_in, 2 + i)
-    go(y_copies[8])
 
     for src, dst in ((q_in, qp), (k_in, kp), (v_in, vp)):
         pack(src, dst, 0)
@@ -350,22 +346,32 @@
 
     x_start(0, 0)
     x_start(0, 1)
+    loads[3].wait()
+    for i in range(2):
+        grad_out[pl.ds(i * BLOCK, BLOCK), :] = pick_block(g_in, 2 + i)
+    go(y_copies[8])
+    go(y_copies[9])
 
     subs = [(1, NX), (NX, 2 * NX)]
-    last_step = {("r", 0): half - 1, ("r", 1): half - 2, ("l", 0): half - 2, ("l", 1): half - 1}
 
     def w_piece(sub, at):
         first, end = subs[sub]
         return w_all.at[pl.ds(first, end - first), piece_rows(at), :]
 
+    def to_sibling(sub, number, at):
+        sem = sub * nz + number
+        return remote(w_piece(sub, at), w_piece(sub, at), s_send.at[sem], s_recv.at[sem], sibling)
+
     z_copies = {}
     s_copies = {}
     for sub in range(2):
-        s_copies["own", sub, 0] = (sub * nz, z)
-        for way in ("r", "l"):
-            for s in range(last_step[way, sub] + 1):
+        s_copies["near", sub, 0] = to_sibling(sub, 0, z)
+        s_copies["far", sub, 0] = to_sibling(sub, 1, (z + half) % nz)
+        for n, way in enumerate(("r", "l")):
+            for s in range(half - 1):
                 at = (z + nz - s) % nz if way == "r" else (z + s) % nz
-                sem = ((0 if way == "r" else 1) * 2 + sub) * half + s
+                came = (z + nz - s - 1) % nz if way == "r" else (z + s + 1) % nz
+                sem = (n * 2 + sub) * half + s
                 z_copies[way, sub, s] = remote(
                     w_piece(sub, at),
                     w_piece(sub, at),
@@ -373,38 +379,38 @@
                     z_recv.at[sem],
                     z_right if way == "r" else z_left,
                 )
-                came = (z + nz - s - 1) % nz if way == "r" else (z + s + 1) % nz
-                number = 1 + s if way == "r" else half + 1 + s
-                if way == "l" and sub == 1:
-                    number = half + s
-                s_copies[way, sub, s] = (sub * nz + number, came)
-    for key, (sem, at) in list(s_copies.items()):
-        sub = key[1]
-        s_copies[key] = remote(w_piece(sub, at), w_piece(sub, at), s_send.at[sem], s_recv.at[sem], sibling)
-
-    def ring_start(sub):
+                s_copies[way, sub, s] = to_sibling(sub, 2 + n * (half - 1) + s, came)
+
+    def fetched(way, sub):
         first, end = subs[sub]
         for slot in range(first, end):
-            fetches[slot].wait_recv()
+            fetches[way, slot].wait_recv()
+
+    def ring_start(sub):
+        fetched("near", sub)
         for way in ("r", "l"):
             if (way, sub, 0) in z_copies:
                 go(z_copies[way, sub, 0])
-        go(s_copies["own", sub, 0])
+        go(s_copies["near", sub, 0])
 
     def ring_step(sub, s):
+        if s >= half - 1:
+            return
         for way in ("r", "l"):
-            if (way, sub, s) in z_copies:
-                z_copies[way, sub, s].wait_recv()
-                if (way, sub, s + 1) in z_copies:
-                    go(z_copies[way, sub, s + 1])
-                go(s_copies[way, sub, s])
-
-    steps = [(sub, s) for s in range(half) for sub in range(2)]
-
-    def ring_steps(count):
-        for _ in range(count):
-            if steps:
-                ring_step(*steps.pop(0))
+            z_copies[way, sub, s].wait_recv()
+            if (way, sub, s + 1) in z_copies:
+                go(z_copies[way, sub, s + 1])
+        for way in ("r", "l"):
+            go(s_copies[way, sub, s])
+
+    def far_arrived(sub):
+        fetched("far", sub)
+        go(s_copies["far", sub, 0])
+
+    def sub_complete(sub):
+        for key, copy in s_copies.items():
+            if key[1] == sub:
+                copy.wait_recv()
 
     def y_arrived(i):
         y_copies[i].wait_recv()
@@ -420,60 +426,71 @@
             acc[rows, lanes] = total
 
     ring_start(0)
+    for slot in fetch_order:
+        go(fetches["far", slot])
     for i in range(2):
         live_grad(i, pick_block(g_in, i))
-    backward(0)
+    backward(0, range(0, heads - 1))
+    x_relay(0, 0)
+    x_relay(0, 1)
+    backward(0, range(heads - 1, heads))
     store_grads(0)
     ring_start(1)
-    x_relay(0, 0)
-    x_relay(0, 1)
-    ring_steps(1)
+    ring_step(0, 0)
     y_arrived(0)
     x_start(1, 0)
     y_arrived(2)
     x_start(2, 0)
-    ring_steps(2)
+    ring_step(1, 0)
+    ring_step(0, 1)
     x_relay(1, 0)
     x_relay(2, 0)
     y_arrived(1)
     x_start(1, 1)
     y_arrived(3)
     x_start(2, 1)
-    ring_steps(2)
-    x_relay(1, 1)
-    x_relay(2, 1)
-    ring_steps(1)
+    ring_step(1, 1)
     y_arrived(4)
     go(y_copies[6])
     y_arrived(5)
     go(y_copies[7])
-    go(y_copies[9])
-    loads[4].wait()
-    project(0, [0], True)
-    project(1, [0], True)
-    ring_steps(2)
+    ring_step(0, 2)
+    x_relay(1, 1)
+    x_relay(2, 1)
+    far_arrived(0)
+    far_arrived(1)
+    y_arrived(8)
+    y_arrived(9)
+    for i in range(2):
+        live_grad(2 + i, grad_arrived[pl.ds(i * BLOCK, BLOCK), :])
+    ring_step(1, 2)
+    backward(1, range(0, 1))
+    ring_step(0, 3)
     y_arrived(6)
     x_start(3, 0)
     y_arrived(7)
     x_start(3, 1)
-    ring_steps(2)
+    backward(1, range(1, min(2, heads)))
+    ring_step(1, 3)
     x_relay(3, 0)
     x_relay(3, 1)
-    ring_steps(1)
-    y_arrived(8)
-    y_arrived(9)
-    for i in range(2):
-        live_grad(2 + i, grad_arrived[pl.ds(i * BLOCK, BLOCK), :])
-    backward(1)
+    backward(1, range(2, heads))
     store_grads(1)
-    ring_steps(2 * half)
-    for copy in s_copies.values():
-        copy.wait_recv()
+    loads[4].wait()
+    project(0, [0], True)
+    project(1, [0], True)
+    ring_step(0, 4)
+    for s in range(5, half):
+        ring_step(0, s)
     x_finish(0)
+    x_finish(1)
+    sub_complete(0)
     project(0, [1, 2, 3], False)
-    x_finish(1)
     project(1, [1, 2, 3], False)
+    for s in range(4, half):
+        ring_step(1, s)
     x_finish(2)
+    sub_complete(1)
     project(1, [4, 5, 6, 7], False)
     packed_out[pl.ds(PAIR, PAIR), :] = acc[pl.ds(PAIR, PAIR), :].astype(BF16)
     late = pltpu.make_async_copy(
@@ -549,8 +566,8 @@
             dma((10,)),
             dma((24,)),
             dma((24,)),
-            dma((8,)),
-            dma((8,)),
+            dma((4 * NX,)),
+            dma((4 * NX,)),
             dma((4 * half,)),
             dma((4 * half,)),
             dma((2 * nz,)),

time: 66.6 us -> 65.4 us (0.982)
  Pallas kernels: 65.7 us -> 64.6 us
    pallas_call x1, Pallas kernels: 62.8 us -> 61.7 us  [on_device(): pl.pallas_call(functools.partial(main_kernel, nz), out_shape=(wide, narro...]
where the time goes in v3:
time: 65.4 us; the launch traced here: 65.2 us
  Pallas kernels  64.6 us (99%)
    pallas_call x1, Pallas kernels, on_device(): pl.pallas_call(functools.partial(main_kernel, nz), out_shape=(wide, narro...  61.7 us
    pallas_call x1, Pallas kernels, on_device(): pl.pallas_call(place_kernel, out_shape=(wide, narrow, narrow, narrow), in...  2.89 us

profile of v3, /device:TPU:1, one launch (start us, length us, event | category | flops | bytes accessed | tf_op | source)
XLA Modules:
  0.0 65.2 jit_solution(8048739305241067752)
XLA Ops:
  0.6 61.7 %attend_gather_project.1 = (bf16[512,768]{1,0:T(8,128)(2,1)}, bf16[512,384]{1,0:T(8,128)(2,1)}, bf16[512,384]{1,0:T(8,128)(2,1)}, bf16[512,384]{1,0:T(8,128)(2,1)}) custom-call(s32[4]{0:T(128)} %send_ref.3, s32[4,128]{1,0:T(4,128)} %bitcast.1, bf16[512,384]{1,0:T(8,128)(2,1)} %q_hbm.1, bf16[512,384]{1,0:T(8,128)(2,1)} %k_hbm.1, bf16[512,384]{1,0:T(8,128)(2,1)} %v_hbm.1, ...), custom_call_target="tpu_custom_call" | custom-call | tf_op jit(solution)/shard_map/attend_gather_project/pallas_call | solution.py:537
  62.3 2.9 %place_blocks.1 = (bf16[512,768]{1,0:T(8,128)(2,1)}, bf16[512,384]{1,0:T(8,128)(2,1)}, bf16[512,384]{1,0:T(8,128)(2,1)}, bf16[512,384]{1,0:T(8,128)(2,1)}) custom-call(s32[4]{0:T(128)} %send_ref.3, bf16[512,768]{1,0:T(8,128)(2,1)} %get-tuple-element.8.out_p, bf16[512,384]{1,0:T(8,128)(2,1)} %get-tuple-element.9.dq_p, ...), custom_call_target="tpu_custom_call" | custom-call | tf_op jit(solution)/shard_map/place_blocks/pallas_call | solution.py:589
